TPU v7x, 32 devices: a whole 2x2x4 slice. The times are simulated.
32 devices in a mesh: shot: 2 (over y), gx: 16 (over z, x, core).
Axes of the slice: x: 2, y: 2, z: 4, core: 2. Of those that a mesh axis runs over, the one named last changes fastest.
Arguments:
- wave_now: float32 [4, 128, 16, 128], P('shot', 'gx'), parts along dimension 0, may hold values from -6 to 6
- wave_prev: float32 [4, 128, 16, 128], P('shot', 'gx'), parts along dimension 0, may hold values from -6 to 6
- speed_term: float32 [128, 16, 128], P('gx'), may hold values from 0.02 to 0.07
- thomsen_epsilon: float32 [128, 16, 128], P('gx'), may hold values from 0.15 to 0.35
- thomsen_delta: float32 [128, 16, 128], P('gx'), may hold values from 0 to 0.1
- tilt_angle: float32 [128, 16, 128], P('gx'), may hold values from -3.140625 to 3.140625
- source_store: bfloat16 [4, 4, 128, 16, 128], P('shot', None, None, 'gx'), parts along dimension 0, may hold values from -6 to 6
- receiver_row: int32 [256], P('shot'), parts along dimension 0, may hold values from 0 to 127
- receiver_column: int32 [256], P('shot'), parts along dimension 0, may hold values from 0 to 15
- receiver_traces: float32 [8, 128], P('shot'), parts along dimension 0, may hold values from -12 to 12
- angle_table: int32 [32], replicated, may hold values from 0 to 7, as said below
Outputs:
- angle_images: bfloat16 [16, 128, 16, 128], P('shot', 'gx'), parts along dimension 0
- wave_final: float32 [4, 128, 16, 128], P('shot', 'gx'), parts along dimension 0
There are 2 independent parts, one for each index of `shot`. A program takes and returns all parts, laid end to end along the dimension named above; an argument that names none is the same for every part. Nothing has to cross between parts.
Inputs may be any that keep to these rules, and one draw needn't show every extreme that they name: angle_table is non-decreasing: angle_table[f] <= angle_table[f+1] for every fine bin f, and every one of the 8 angle images is named by at least one fine bin.
All inputs are finite; a program needn't handle non-finite values.
Results may differ from a plain program's by a relative error of at most 0.001.
Values may be sent and summed in bfloat16 or wider, within the bound.
A program may use at most 128 MiB of HBM per device.

v0:
```python
import jax
import jax.numpy as jnp
from jax import lax
from jax.sharding import PartitionSpec as P

STEPS = 4
IMAGE_EVERY = 2
NBIN = 8
FINE = 32
REC_DEPTH = 2


second_coeffs = (-205.0 / 72.0, 8.0 / 5.0, -1.0 / 5.0, 8.0 / 315.0, -1.0 / 560.0)
first_coeffs = (4.0 / 5.0, -1.0 / 5.0, 4.0 / 105.0, -1.0 / 280.0)
stencil_reach = 4


def padded_2(cells, sides, width):
    for axis, dim in sides:
        count = lax.axis_size(axis)
        ends = count - 1
        head = lax.slice_in_dim(cells, 0, width, axis=dim)
        tail = lax.slice_in_dim(cells, cells.shape[dim] - width, cells.shape[dim], axis=dim)
        cells = jnp.concatenate(
            [
                lax.ppermute(tail, axis, [(i, (i + 1) % count) for i in range(ends)]),
                cells,
                lax.ppermute(head, axis, [((i + 1) % count, i) for i in range(ends)]),
            ],
            axis=dim,
        )
    return cells


def window(array_in, direction, begin_at, extent):
    return lax.slice_in_dim(array_in, begin_at, begin_at + extent, axis=direction)


def moved(field, direction, offset):
    length = field.shape[direction]
    shape = list(field.shape)
    shape[direction] = abs(offset)
    zeros = jnp.zeros(tuple(shape), field.dtype)
    if offset > 0:
        return jnp.concatenate(
            [lax.slice_in_dim(field, offset, length, axis=direction), zeros], axis=direction
        )
    return jnp.concatenate(
        [zeros, lax.slice_in_dim(field, 0, length + offset, axis=direction)], axis=direction
    )


def second_along(field, direction):
    summed = second_coeffs[0] * field
    for offset in range(1, 5):
        summed = summed + second_coeffs[offset] * (
            moved(field, direction, offset) + moved(field, direction, -offset)
        )
    return summed


def first_along(field, direction):
    summed = first_coeffs[0] * (moved(field, direction, 1) - moved(field, direction, -1))
    for offset in range(2, 5):
        summed = summed + first_coeffs[offset - 1] * (
            moved(field, direction, offset) - moved(field, direction, -offset)
        )
    return summed


def second_diff(padded, direction, extent):
    summed = second_coeffs[0] * window(padded, direction, stencil_reach, extent)
    for offset in range(1, 5):
        summed = summed + second_coeffs[offset] * (
            window(padded, direction, stencil_reach + offset, extent)
            + window(padded, direction, stencil_reach - offset, extent)
        )
    return summed


def first_diff(padded, direction, extent):
    summed = first_coeffs[0] * (
        window(padded, direction, stencil_reach + 1, extent)
        - window(padded, direction, stencil_reach - 1, extent)
    )
    for offset in range(2, 5):
        summed = summed + first_coeffs[offset - 1] * (
            window(padded, direction, stencil_reach + offset, extent)
            - window(padded, direction, stencil_reach - offset, extent)
        )
    return summed


def advance(padded, earlier, medium, traces_now, receiver_row, receiver_column, first_row):
    extent_x = earlier.shape[1]
    extent_y = earlier.shape[2]
    speed, epsilon, thomsen, tilt = medium
    second_x = second_diff(padded, 1, extent_x)
    inner_rows = padded[:, 4:-4]
    second_y = second_along(inner_rows[0], 1)
    second_z = second_along(inner_rows, 3)
    slope_z_all = first_along(padded, 3)
    mixed = first_diff(slope_z_all, 1, extent_x)
    slope_x = first_diff(padded[0], 0, extent_x)
    slope_y = first_along(inner_rows[0], 1)
    slope_z = slope_z_all[0, 4:-4]
    cosine = jnp.cos(tilt)
    sine = jnp.sin(tilt)
    rotated = cosine * cosine * second_z + sine * sine * second_x + 2.0 * sine * cosine * mixed
    across_p = second_x[0] + second_y + second_z[0] - rotated[0]
    ratio = jnp.sqrt(1.0 + 2.0 * thomsen)
    p_next = (
        2.0 * inner_rows[0]
        - earlier[0]
        + speed * ((1.0 + 2.0 * epsilon) * across_p + ratio * rotated[1])
    )
    q_next = 2.0 * inner_rows[1] - earlier[1] + speed * (ratio * across_p + rotated[1])
    local_row = receiver_row - first_row
    inside = (local_row >= 0) & (local_row < extent_x)
    flat_index = jnp.where(inside, local_row * extent_y + receiver_column, extent_x * extent_y)
    plane = (
        jnp.zeros((extent_x * extent_y,), jnp.float32).at[flat_index].add(traces_now, mode="drop")
    )
    p_next = p_next.at[:, :, REC_DEPTH].add(plane.reshape(extent_x, extent_y))
    return (jnp.stack([p_next, q_next]), (slope_x, slope_y, slope_z))


def angle_image(snapshot, wave_field, earlier_field, slopes, bounds):
    lower, upper = bounds
    rate = wave_field - earlier_field
    flux_x = -rate * slopes[0]
    flux_y = -rate * slopes[1]
    flux_z = -rate * slopes[2]
    inner = snapshot[1] * flux_x + snapshot[2] * flux_y + snapshot[3] * flux_z
    lengths = jnp.sqrt(
        snapshot[1] * snapshot[1] + snapshot[2] * snapshot[2] + snapshot[3] * snapshot[3]
    ) * jnp.sqrt(flux_x * flux_x + flux_y * flux_y + flux_z * flux_z)
    cosine = inner / jnp.maximum(lengths, 1.0)
    scaled = (cosine + 1.0) * (0.5 * (FINE - 1))
    shaped = (lower.shape[0],) + (1,) * scaled.ndim
    rising = jnp.clip(scaled[None] - lower.reshape(shaped) + 1.0, 0.0, 1.0)
    falling = jnp.clip(upper.reshape(shaped) + 1.0 - scaled[None], 0.0, 1.0)
    return jnp.minimum(rising, falling) * (snapshot[0] * wave_field)[None]


def local(
    wave_now,
    wave_prev,
    speed_term,
    thomsen_epsilon,
    thomsen_delta,
    tilt_angle,
    source_store,
    receiver_row,
    receiver_column,
    receiver_traces,
    angle_table,
):
    extent_x = wave_now.shape[1]
    first_row = lax.axis_index("gx") * extent_x
    image_ids = jnp.arange(NBIN, dtype=jnp.int32)[:, None]
    lower = jnp.sum((angle_table[None, :] < image_ids).astype(jnp.float32), axis=1)
    upper = jnp.sum((angle_table[None, :] <= image_ids).astype(jnp.float32), axis=1) - 1.0
    bounds = (lower, upper)
    medium = (speed_term, thomsen_epsilon, thomsen_delta, tilt_angle)
    arrived = lax.all_to_all(source_store, "gx", split_axis=2, concat_axis=3, tiled=True)
    images = jnp.zeros((NBIN,) + wave_now.shape[1:], jnp.float32)
    current = wave_now
    earlier = wave_prev
    for time_step in range(STEPS):
        padded = padded_2(current, (("gx", 1),), 4)
        following, slopes = advance(
            padded,
            earlier,
            medium,
            receiver_traces[time_step],
            receiver_row,
            receiver_column,
            first_row,
        )
        if time_step % IMAGE_EVERY == IMAGE_EVERY - 1:
            snap_index = time_step // IMAGE_EVERY
            snapshot = arrived[snap_index]
            images = images + angle_image(
                snapshot.astype(jnp.float32), current[0], earlier[0], slopes, bounds
            )
        earlier = current
        current = following
    return (images.astype(jnp.bfloat16), current)


def solution(mesh):
    placed = (
        P("shot", "gx", None, None),
        P("shot", "gx", None, None),
        P("gx", None, None),
        P("gx", None, None),
        P("gx", None, None),
        P("gx", None, None),
        P("shot", None, None, "gx", None),
        P("shot"),
        P("shot"),
        P("shot", None),
        P(),
    )
    return jax.shard_map(
        local,
        mesh=mesh,
        in_specs=placed,
        out_specs=(P("shot", "gx", None, None), P("shot", "gx", None, None)),
        check_vma=False,
    )
```

profile of v0, /device:TPU:1, one launch (start us, length us, event | category | flops | bytes accessed | tf_op | source)
XLA Modules:
  0.0 364.0 jit_solution(14505903367550043758)
XLA Ops:
  2.2 4.5 %collective-permute-start.1 = (f32[2,4,16,128]{3,2,1,0:T(8,128)}, f32[2,4,16,128]{3,2,1,0:T(8,128)}, u32[]{:S(2)}, u32[]{:S(2)}) collective-permute-start(f32[2,4,16,128]{3,2,1,0:T(8,128)} %get-tuple-element.268), channel_id=1, source_target_pairs={{0,1},{1,2},{2,3},{3,4},{4,5},{5,6},{6,7},{7,8},{8,9},{9,10},{10,1... | collective-permute-start | bytes 196616 | tf_op jit(solution)/shard_map/ppermute | solution.py:26
  10.5 6.5 %all-to-all-start = ((bf16[2,4,128,1,128]{4,1,0,3,2:T(4,128)(2,1)}), bf16[2,4,128,1,128]{4,1,0,3,2:T(4,128)(2,1)}, u32[]{:S(2)}, u32[]{:S(2)}) async-start(bf16[2,4,128,1,128]{4,1,0,3,2:T(4,128)(2,1)} %copy.520), calls=%async_computation | async-start | bytes 524288 | tf_op jit(solution)/shard_map/all_to_all | solution.py:166
  30.3 2.6 fusion.168
  49.7 3.1 copy.635
  52.7 3.1 copy.634
  55.8 3.1 copy.633
  59.0 3.0 copy.632
  62.0 2.2 copy.631
  64.2 3.1 copy.630
  67.3 3.1 copy.629
  73.2 2.3 copy.534
  76.2 2.3 copy.535
  86.6 6.5 %multiply_add_fusion.3 = f32[2,16,16,128]{2,1,3,0:T(8,128)S(1)} fusion(f32[2,16,16,124]{2,1,3,0:T(8,128)} %copy.635, f32[2,16,16,124]{2,1,3,0:T(8,128)} %copy.634, f32[2,16,16,125]{2,1,3,0:T(8,128)} %copy.633, f32[2,16,16,125]{2,1,3,0:T(8,128)} %copy.632, f32[2,16,16,126]{2,1,3,0:T(8,128)} %copy.631, f32[2,16,16,126]{2,1,3,0:T(8,128)} %copy.630, ...), kind=kLoop, calls=%fused_computation.73 | loop fusion | flops 720896 | bytes 2318336 | tf_op jit(solution)/shard_map/add | solution.py:65
  95.9 5.0 %fusion.30 = (f32[2,8,16,128]{2,1,3,0:T(8,128)S(1)}, f32[2,8,16,128]{2,1,3,0:T(8,128)}, f32[2,8,16,128]{2,1,3,0:T(8,128)}) fusion(f32[2,16,16,128]{2,1,3,0:T(8,128)S(1)} %multiply_add_fusion.3, f32[8,16,128]{1,0,2:T(8,128)S(1)} %get-tuple-element.146, f32[8,16,128]{1,0,2:T(8,128)S(1)} %copy-done.19, f32[8,16,128]{1,0,2:T(8,128)S(1)} %copy-done.23, ...), kind=kLoop, calls=%fused_computation.118 | loop fusion | flops 1343488 | bytes 3846144 | tf_op jit(solution)/shard_map/add | solution.py:109
  100.8 3.4 fusion.82
  118.2 3.7 %collective-permute-start.3 = (f32[2,4,16,128]{2,1,3,0:T(4,128)}, f32[2,4,16,128]{2,1,3,0:T(4,128)}, u32[]{:S(2)}, u32[]{:S(2)}) collective-permute-start(f32[2,4,16,128]{2,1,3,0:T(4,128)} %get-tuple-element.136), channel_id=1, source_target_pairs={{0,1},{1,2},{2,3},{3,4},{4,5},{5,6},{6,7},{7,8},{8,9},{9,10},{10,1... | collective-permute-start | bytes 196616 | tf_op jit(solution)/shard_map/ppermute | solution.py:26
  124.5 2.4 collective-permute-done.2
  126.8 6.1 %collective-permute-done.3 = f32[2,4,16,128]{2,1,3,0:T(4,128)} collective-permute-done((f32[2,4,16,128]{2,1,3,0:T(4,128)}, f32[2,4,16,128]{2,1,3,0:T(4,128)}, u32[]{:S(2)}, u32[]{:S(2)}) %collective-permute-start.3) | collective-permute-done | bytes 65568 | tf_op jit(solution)/shard_map/ppermute | solution.py:26
  134.4 2.4 fusion.147
  136.8 2.3 fusion.146
  139.1 2.3 fusion.145
  141.4 2.4 fusion.144
  145.9 2.2 copy.581
  148.1 2.3 copy.582
  159.3 6.5 %multiply_add_fusion.2 = f32[2,16,16,128]{2,1,3,0:T(8,128)S(1)} fusion(f32[2,16,16,124]{2,1,3,0:T(8,128)} %get-tuple-element.107, f32[2,16,16,124]{2,1,3,0:T(8,128)} %get-tuple-element.106, f32[2,16,16,125]{2,1,3,0:T(8,128)} %get-tuple-element.105, f32[2,16,16,125]{2,1,3,0:T(8,128)} %get-tuple-element.104, f32[2,16,16,126]{2,1,3,0:T(8,128)} %get-tuple-element.103, ...), kind=kLoop, calls=%fused_computation.72 | loop fusion | flops 720896 | bytes 2318336 | tf_op jit(solution)/shard_map/add | solution.py:65
  168.1 6.3 %fusion.21 = (f32[2,8,16,128]{2,1,3,0:T(8,128)S(1)}, f32[2,8,16,128]{2,1,3,0:T(8,128)}, f32[2,8,16,128]{2,1,3,0:T(8,128)}) fusion(f32[2,16,16,128]{2,1,3,0:T(8,128)S(1)} %multiply_add_fusion.2, f32[8,16,128]{1,0,2:T(8,128)S(1)} %copy-done.16, f32[8,16,128]{1,0,2:T(8,128)S(1)} %copy-done.20, f32[8,16,128]{1,0,2:T(8,128)S(1)} %copy-done.24, ...), kind=kLoop, calls=%fused_computation.104 | loop fusion | flops 1376256 | bytes 3846144 | tf_op jit(solution)/shard_map/add | solution.py:109
  192.9 4.6 %collective-permute-start.5 = (f32[2,4,16,128]{2,1,3,0:T(4,128)}, f32[2,4,16,128]{2,1,3,0:T(4,128)}, u32[]{:S(2)}, u32[]{:S(2)}) collective-permute-start(f32[2,4,16,128]{2,1,3,0:T(4,128)} %get-tuple-element.126), channel_id=1, source_target_pairs={{0,1},{1,2},{2,3},{3,4},{4,5},{5,6},{6,7},{7,8},{8,9},{9,10},{10,1... | collective-permute-start | bytes 196616 | tf_op jit(solution)/shard_map/ppermute | solution.py:26
  213.0 2.4 fusion.143
  215.4 2.3 fusion.142
  217.7 2.3 fusion.141
  220.0 2.3 fusion.140
  230.1 2.3 copy.596
  232.3 2.3 copy.593
  243.1 6.5 %multiply_add_fusion.1 = f32[2,16,16,128]{2,1,3,0:T(8,128)S(1)} fusion(f32[2,16,16,124]{2,1,3,0:T(8,128)} %get-tuple-element.99, f32[2,16,16,124]{2,1,3,0:T(8,128)} %get-tuple-element.98, f32[2,16,16,125]{2,1,3,0:T(8,128)} %get-tuple-element.97, f32[2,16,16,125]{2,1,3,0:T(8,128)} %get-tuple-element.96, f32[2,16,16,126]{2,1,3,0:T(8,128)} %get-tuple-element.95, ...), kind=kLoop, calls=%fused_computation.71 | loop fusion | flops 720896 | bytes 2318336 | tf_op jit(solution)/shard_map/add | solution.py:65
  251.9 5.4 %fusion.12 = (f32[2,8,16,128]{2,1,3,0:T(8,128)S(1)}, f32[2,8,16,128]{2,1,3,0:T(8,128)}, f32[2,8,16,128]{2,1,3,0:T(8,128)}) fusion(f32[2,16,16,128]{2,1,3,0:T(8,128)S(1)} %multiply_add_fusion.1, f32[8,16,128]{1,0,2:T(8,128)S(1)} %copy-done.17, f32[8,16,128]{1,0,2:T(8,128)S(1)} %copy-done.21, f32[8,16,128]{1,0,2:T(8,128)S(1)} %copy-done.25, ...), kind=kLoop, calls=%fused_computation.91 | loop fusion | flops 1376256 | bytes 3846144 | tf_op jit(solution)/shard_map/add | solution.py:109
  258.3 4.2 %fusion.84 = (f32[1,8,16,128]{2,1,3,0:T(8,128)}, f32[8,16,128]{1,0,2:T(8,128)}) fusion(f32[8,16,128]{1,0,2:T(8,128)S(1)} %copy-done.7, f32[2,8,16,128]{2,1,3,0:T(8,128)S(1)} %get-tuple-element.69, f32[8,16,128]{1,0,2:T(8,128)S(1)} %get-tuple-element.77, f32[8,16,128]{1,0,2:T(8,128)S(1)} %get-tuple-element.72, f32[8,16,128]{1,0,2:T(8,128)S(1)} %copy-done.12, ...), kind=kLoop, calls=%fused_computation.254 | loop fusion | flops 360448 | bytes 1163264 | tf_op jit(solution)/shard_map/stack | solution.py:125
  262.4 3.3 copy.522
  265.8 3.3 slice_convert_fusion.1
  283.8 3.9 %collective-permute-start.7 = (f32[2,4,16,128]{2,1,3,0:T(4,128)}, f32[2,4,16,128]{2,1,3,0:T(4,128)}, u32[]{:S(2)}, u32[]{:S(2)}) collective-permute-start(f32[2,4,16,128]{2,1,3,0:T(4,128)} %get-tuple-element.116), channel_id=1, source_target_pairs={{0,1},{1,2},{2,3},{3,4},{4,5},{5,6},{6,7},{7,8},{8,9},{9,10},{10,1... | collective-permute-start | bytes 196616 | tf_op jit(solution)/shard_map/ppermute | solution.py:26
  287.8 3.4 add_multiply_fusion.1
  299.1 2.3 fusion.139
  301.4 2.3 fusion.138
  303.7 2.3 fusion.137
  306.0 2.3 fusion.136
  322.4 6.8 %multiply_add_fusion = f32[2,16,16,128]{2,1,3,0:T(8,128)S(1)} fusion(f32[2,16,16,124]{2,1,3,0:T(8,128)} %get-tuple-element.91, f32[2,16,16,124]{2,1,3,0:T(8,128)} %get-tuple-element.90, f32[2,16,16,125]{2,1,3,0:T(8,128)} %get-tuple-element.89, f32[2,16,16,125]{2,1,3,0:T(8,128)} %get-tuple-element.88, f32[2,16,16,126]{2,1,3,0:T(8,128)} %get-tuple-element.87, ...), kind=kLoop, calls=%fused_computation.70 | loop fusion | flops 720896 | bytes 2318336 | tf_op jit(solution)/shard_map/add | solution.py:65
  330.9 6.3 %fusion.3 = (f32[2,8,16,128]{2,1,3,0:T(8,128)S(1)}, f32[2,8,16,128]{2,1,3,0:T(8,128)}, f32[2,8,16,128]{2,1,3,0:T(8,128)}) fusion(f32[2,16,16,128]{2,1,3,0:T(8,128)S(1)} %multiply_add_fusion, f32[8,16,128]{1,0,2:T(8,128)S(1)} %copy-done.18, f32[8,16,128]{1,0,2:T(8,128)S(1)} %copy-done.22, f32[8,16,128]{1,0,2:T(8,128)S(1)} %copy-done.26, ...), kind=kLoop, calls=%fused_computation.78 | loop fusion | flops 1376256 | bytes 3846144 | tf_op jit(solution)/shard_map/add | solution.py:109
  337.3 3.6 multiply_add_fusion.12
  351.6 6.4 %add_multiply_fusion = f32[8,16,128]{1,0,2:T(8,128)} fusion(f32[1,4,8,16,1,128]{3,2,5,4,1,0:T(8,128)} %get-tuple-element.83, f32[2,16,16,128]{2,1,3,0:T(8,128)} %copy-done.3, f32[1,8,16,128]{2,1,3,0:T(8,128)} %copy.609, f32[1,8,16,128]{2,1,3,0:T(8,128)} %copy.610, f32[1,8,16,128]{2,1,3,0:T(8,128)} %copy.607, f32[1,8,16,128]{2,1,3,0:T(8,128)} %copy.608, ...), kind=kLoop, calls=%fused_computation.219 | loop fusion | flops 770048 | bytes 1425408 | tf_op jit(solution)/shard_map/mul | solution.py:139
  (423 shorter events, 188.2 us)
Async XLA Ops:
  2.2 43.1 %collective-permute-start.1 = (f32[2,4,16,128]{3,2,1,0:T(8,128)}, f32[2,4,16,128]{3,2,1,0:T(8,128)}, u32[]{:S(2)}, u32[]{:S(2)}) collective-permute-start(f32[2,4,16,128]{3,2,1,0:T(8,128)} %get-tuple-element.268), channel_id=1, source_target_pairs={{0,1},{1,2},{2,3},{3,4},{4,5},{5,6},{6,7},{7,8},{8,9},{9,10},{10,1... | collective-permute-start | bytes 196616 | tf_op jit(solution)/shard_map/ppermute | solution.py:26
  6.7 39.5 %collective-permute-start = (f32[2,4,16,128]{3,2,1,0:T(8,128)}, f32[2,4,16,128]{3,2,1,0:T(8,128)S(1)}, u32[]{:S(2)}, u32[]{:S(2)}) collective-permute-start(f32[2,4,16,128]{3,2,1,0:T(8,128)} %get-tuple-element.267), channel_id=1, source_target_pairs={{1,0},{2,1},{3,2},{4,3},{5,4},{6,5},{7,6},{8,7},{9,8},{10,9},{11,1... | collective-permute-start | bytes 196616 | tf_op jit(solution)/shard_map/ppermute | solution.py:28
  10.5 252.0 %all-to-all-start = ((bf16[2,4,128,1,128]{4,1,0,3,2:T(4,128)(2,1)}), bf16[2,4,128,1,128]{4,1,0,3,2:T(4,128)(2,1)}, u32[]{:S(2)}, u32[]{:S(2)}) async-start(bf16[2,4,128,1,128]{4,1,0,3,2:T(4,128)(2,1)} %copy.520), calls=%async_computation | async-start | bytes 524288 | tf_op jit(solution)/shard_map/all_to_all | solution.py:166
  29.0 145.4 %copy-start.6 = (f32[8,16,128]{1,0,2:T(8,128)}, f32[8,16,128]{1,0,2:T(8,128)S(1)}, u32[]{:S(2)}) copy-start(f32[8,16,128]{1,0,2:T(8,128)S(1)} %copy.557) | copy-start | bytes 196612
  33.1 71.1 %copy-start.10 = (f32[8,16,128]{1,0,2:T(8,128)}, f32[8,16,128]{1,0,2:T(8,128)S(1)}, u32[]{:S(2)}) copy-start(f32[8,16,128]{1,0,2:T(8,128)S(1)} %copy.556) | copy-start | bytes 196612
  33.1 11.4 %copy-start.130 = (s32[32]{0:T(128)S(1)}, s32[32]{0:T(128)}, u32[]{:S(2)}) copy-start(s32[32]{0:T(128)} %param.29) | copy-start | bytes 388
  33.1 13.0 %copy-start.103 = (f32[2,8,16,128]{3,2,1,0:T(8,128)S(1)}, f32[2,8,16,128]{3,2,1,0:T(8,128)}, u32[]{:S(2)}) copy-start(f32[2,8,16,128]{3,2,1,0:T(8,128)} %param.19) | copy-start | bytes 393220
  44.5 48.6 %copy-start.15 = (f32[8,16,128]{1,0,2:T(8,128)}, f32[8,16,128]{1,0,2:T(8,128)S(1)}, u32[]{:S(2)}) copy-start(f32[8,16,128]{1,0,2:T(8,128)S(1)} %get-tuple-element.146) | copy-start | bytes 196612
  86.5 8.1 %copy-start.85 = (f32[2,8,16,128]{2,1,3,0:T(8,128)S(1)}, f32[2,8,16,128]{2,1,3,0:T(8,128)}, u32[]{:S(2)}) copy-start(f32[2,8,16,128]{2,1,3,0:T(8,128)} %copy.528) | copy-start | bytes 393220
  86.5 8.4 %copy-start.86 = (f32[2,8,16,128]{2,1,3,0:T(8,128)S(1)}, f32[2,8,16,128]{2,1,3,0:T(8,128)}, u32[]{:S(2)}) copy-start(f32[2,8,16,128]{2,1,3,0:T(8,128)} %copy.529) | copy-start | bytes 393220
  86.5 8.7 %copy-start.88 = (f32[2,8,16,127]{2,1,3,0:T(8,128)S(1)}, f32[2,8,16,127]{2,1,3,0:T(8,128)}, u32[]{:S(2)}) copy-start(f32[2,8,16,127]{2,1,3,0:T(8,128)} %get-tuple-element.138) | copy-start | bytes 390148
  86.6 9.0 %copy-start.89 = (f32[2,8,16,127]{2,1,3,0:T(8,128)S(1)}, f32[2,8,16,127]{2,1,3,0:T(8,128)}, u32[]{:S(2)}) copy-start(f32[2,8,16,127]{2,1,3,0:T(8,128)} %get-tuple-element.139) | copy-start | bytes 390148
  86.6 9.3 %copy-start.90 = (f32[2,8,16,126]{2,1,3,0:T(8,128)S(1)}, f32[2,8,16,126]{2,1,3,0:T(8,128)}, u32[]{:S(2)}) copy-start(f32[2,8,16,126]{2,1,3,0:T(8,128)} %get-tuple-element.140) | copy-start | bytes 387076
  116.1 10.7 %collective-permute-start.2 = (f32[2,4,16,128]{2,1,3,0:T(4,128)}, f32[2,4,16,128]{2,1,3,0:T(4,128)S(1)}, u32[]{:S(2)}, u32[]{:S(2)}) collective-permute-start(f32[2,4,16,128]{2,1,3,0:T(4,128)} %get-tuple-element.137), channel_id=1, source_target_pairs={{1,0},{2,1},{3,2},{4,3},{5,4},{6,5},{7,6},{8,7},{9,8},{10,9},{11,1... | collective-permute-start | bytes 196616 | tf_op jit(solution)/shard_map/ppermute | solution.py:28
  118.2 14.7 %collective-permute-start.3 = (f32[2,4,16,128]{2,1,3,0:T(4,128)}, f32[2,4,16,128]{2,1,3,0:T(4,128)}, u32[]{:S(2)}, u32[]{:S(2)}) collective-permute-start(f32[2,4,16,128]{2,1,3,0:T(4,128)} %get-tuple-element.136), channel_id=1, source_target_pairs={{0,1},{1,2},{2,3},{3,4},{4,5},{5,6},{6,7},{7,8},{8,9},{9,10},{10,1... | collective-permute-start | bytes 196616 | tf_op jit(solution)/shard_map/ppermute | solution.py:26
  159.3 8.2 %copy-start.76 = (f32[2,8,16,128]{2,1,3,0:T(8,128)S(1)}, f32[2,8,16,128]{2,1,3,0:T(8,128)}, u32[]{:S(2)}) copy-start(f32[2,8,16,128]{2,1,3,0:T(8,128)} %copy.577) | copy-start | bytes 393220
  159.3 8.7 %copy-start.79 = (f32[2,8,16,128]{2,1,3,0:T(8,128)S(1)}, f32[2,8,16,128]{2,1,3,0:T(8,128)}, u32[]{:S(2)}) copy-start(f32[2,8,16,128]{2,1,3,0:T(8,128)} %copy.578) | copy-start | bytes 393220
  165.9 8.6 %copy-start.2 = (f32[2,16,16,128]{2,1,3,0:T(8,128)}, f32[2,16,16,128]{2,1,3,0:T(8,128)S(1)}, u32[]{:S(2)}) copy-start(f32[2,16,16,128]{2,1,3,0:T(8,128)S(1)} %multiply_add_fusion.2) | copy-start | bytes 786436
  176.7 80.6 %copy-start = (f32[8,16,128]{1,0,2:T(8,128)}, f32[8,16,128]{1,0,2:T(8,128)S(1)}, u32[]{:S(2)}) copy-start(f32[8,16,128]{1,0,2:T(8,128)S(1)} %get-tuple-element.72) | copy-start | bytes 196612
  191.0 20.4 %collective-permute-start.4 = (f32[2,4,16,128]{2,1,3,0:T(4,128)}, f32[2,4,16,128]{2,1,3,0:T(4,128)}, u32[]{:S(2)}, u32[]{:S(2)}) collective-permute-start(f32[2,4,16,128]{2,1,3,0:T(4,128)} %get-tuple-element.127), channel_id=1, source_target_pairs={{1,0},{2,1},{3,2},{4,3},{5,4},{6,5},{7,6},{8,7},{9,8},{10,9},{11,1... | collective-permute-start | bytes 196616 | tf_op jit(solution)/shard_map/ppermute | solution.py:28
  192.9 18.4 %collective-permute-start.5 = (f32[2,4,16,128]{2,1,3,0:T(4,128)}, f32[2,4,16,128]{2,1,3,0:T(4,128)}, u32[]{:S(2)}, u32[]{:S(2)}) collective-permute-start(f32[2,4,16,128]{2,1,3,0:T(4,128)} %get-tuple-element.126), channel_id=1, source_target_pairs={{0,1},{1,2},{2,3},{3,4},{4,5},{5,6},{6,7},{7,8},{8,9},{9,10},{10,1... | collective-permute-start | bytes 196616 | tf_op jit(solution)/shard_map/ppermute | solution.py:26
  199.8 8.4 %copy-start.114 = (f32[1,8,16,128]{3,2,1,0:T(8,128)S(1)}, f32[1,8,16,128]{3,2,1,0:T(8,128)}, u32[]{:S(2)}) copy-start(f32[1,8,16,128]{3,2,1,0:T(8,128)} %get-tuple-element.203) | copy-start | bytes 196612
  199.8 9.4 %copy-start.113 = (f32[1,8,16,128]{3,2,1,0:T(8,128)S(1)}, f32[1,8,16,128]{3,2,1,0:T(8,128)}, u32[]{:S(2)}) copy-start(f32[1,8,16,128]{3,2,1,0:T(8,128)} %get-tuple-element.249) | copy-start | bytes 196612
  199.8 10.4 %copy-start.112 = (f32[1,8,16,128]{3,2,1,0:T(8,128)S(1)}, f32[1,8,16,128]{3,2,1,0:T(8,128)}, u32[]{:S(2)}) copy-start(f32[1,8,16,128]{3,2,1,0:T(8,128)} %get-tuple-element.202) | copy-start | bytes 196612
  230.1 9.0 %copy-start.106 = (f32[2,8,16,128]{3,2,1,0:T(8,128)S(1)}, f32[2,8,16,128]{3,2,1,0:T(8,128)}, u32[]{:S(2)}) copy-start(f32[2,8,16,128]{3,2,1,0:T(8,128)} %get-tuple-element.219) | copy-start | bytes 393220
  243.0 8.3 %copy-start.82 = (f32[2,8,16,128]{2,1,3,0:T(8,128)S(1)}, f32[2,8,16,128]{2,1,3,0:T(8,128)}, u32[]{:S(2)}) copy-start(f32[2,8,16,128]{2,1,3,0:T(8,128)} %copy.589) | copy-start | bytes 393220
  243.1 8.6 %copy-start.84 = (f32[2,8,16,128]{2,1,3,0:T(8,128)S(1)}, f32[2,8,16,128]{2,1,3,0:T(8,128)}, u32[]{:S(2)}) copy-start(f32[2,8,16,128]{2,1,3,0:T(8,128)} %copy.590) | copy-start | bytes 393220
  243.1 8.8 %copy-start.87 = (f32[2,8,16,127]{2,1,3,0:T(8,128)S(1)}, f32[2,8,16,127]{2,1,3,0:T(8,128)}, u32[]{:S(2)}) copy-start(f32[2,8,16,127]{2,1,3,0:T(8,128)} %get-tuple-element.118) | copy-start | bytes 390148
  277.2 10.5 %copy-start.97 = (f32[1,8,16,128]{2,1,3,0:T(8,128)S(1)}, f32[1,8,16,128]{2,1,3,0:T(8,128)}, u32[]{:S(2)}) copy-start(f32[1,8,16,128]{2,1,3,0:T(8,128)} %copy.567) | copy-start | bytes 196612
  277.2 10.5 %copy-start.98 = (f32[1,8,16,128]{2,1,3,0:T(8,128)S(1)}, f32[1,8,16,128]{2,1,3,0:T(8,128)}, u32[]{:S(2)}) copy-start(f32[1,8,16,128]{2,1,3,0:T(8,128)} %copy.568) | copy-start | bytes 196612
  277.2 10.5 %copy-start.99 = (f32[1,8,16,128]{2,1,3,0:T(8,128)S(1)}, f32[1,8,16,128]{2,1,3,0:T(8,128)}, u32[]{:S(2)}) copy-start(f32[1,8,16,128]{2,1,3,0:T(8,128)} %copy.565) | copy-start | bytes 196612
  277.2 10.5 %copy-start.100 = (f32[1,8,16,128]{2,1,3,0:T(8,128)S(1)}, f32[1,8,16,128]{2,1,3,0:T(8,128)}, u32[]{:S(2)}) copy-start(f32[1,8,16,128]{2,1,3,0:T(8,128)} %copy.566) | copy-start | bytes 196612
  278.4 9.4 %copy-start.93 = (f32[1,8,16,128]{2,1,3,0:T(8,128)S(1)}, f32[1,8,16,128]{2,1,3,0:T(8,128)}, u32[]{:S(2)}) copy-start(f32[1,8,16,128]{2,1,3,0:T(8,128)} %copy.571) | copy-start | bytes 196612
  278.4 9.4 %copy-start.94 = (f32[1,8,16,128]{2,1,3,0:T(8,128)S(1)}, f32[1,8,16,128]{2,1,3,0:T(8,128)}, u32[]{:S(2)}) copy-start(f32[1,8,16,128]{2,1,3,0:T(8,128)} %copy.572) | copy-start | bytes 196612
  278.4 9.4 %copy-start.95 = (f32[1,8,16,128]{2,1,3,0:T(8,128)S(1)}, f32[1,8,16,128]{2,1,3,0:T(8,128)}, u32[]{:S(2)}) copy-start(f32[1,8,16,128]{2,1,3,0:T(8,128)} %copy.569) | copy-start | bytes 196612
  278.4 9.4 %copy-start.96 = (f32[1,8,16,128]{2,1,3,0:T(8,128)S(1)}, f32[1,8,16,128]{2,1,3,0:T(8,128)}, u32[]{:S(2)}) copy-start(f32[1,8,16,128]{2,1,3,0:T(8,128)} %copy.570) | copy-start | bytes 196612
  279.5 8.2 %copy-start.36 = (f32[8,12,128]{1,0,2:T(8,128)S(1)}, f32[8,12,128]{1,0,2:T(8,128)}, u32[]{:S(2)}) copy-start(f32[8,12,128]{1,0,2:T(8,128)} %get-tuple-element.174) | copy-start | bytes 147460
  279.5 8.2 %copy-start.38 = (f32[8,12,128]{1,0,2:T(8,128)S(1)}, f32[8,12,128]{1,0,2:T(8,128)}, u32[]{:S(2)}) copy-start(f32[8,12,128]{1,0,2:T(8,128)} %get-tuple-element.175) | copy-start | bytes 147460
  279.5 8.3 %copy-start.40 = (f32[8,13,128]{1,0,2:T(8,128)S(1)}, f32[8,13,128]{1,0,2:T(8,128)}, u32[]{:S(2)}) copy-start(f32[8,13,128]{1,0,2:T(8,128)} %get-tuple-element.172) | copy-start | bytes 159748
  279.5 8.3 %copy-start.42 = (f32[8,13,128]{1,0,2:T(8,128)S(1)}, f32[8,13,128]{1,0,2:T(8,128)}, u32[]{:S(2)}) copy-start(f32[8,13,128]{1,0,2:T(8,128)} %get-tuple-element.173) | copy-start | bytes 159748
  279.5 8.3 %copy-start.44 = (f32[8,14,128]{1,0,2:T(8,128)S(1)}, f32[8,14,128]{1,0,2:T(8,128)}, u32[]{:S(2)}) copy-start(f32[8,14,128]{1,0,2:T(8,128)} %get-tuple-element.170) | copy-start | bytes 172036
  279.5 8.3 %copy-start.46 = (f32[8,14,128]{1,0,2:T(8,128)S(1)}, f32[8,14,128]{1,0,2:T(8,128)}, u32[]{:S(2)}) copy-start(f32[8,14,128]{1,0,2:T(8,128)} %get-tuple-element.171) | copy-start | bytes 172036
  279.6 8.3 %copy-start.48 = (f32[8,15,128]{1,0,2:T(8,128)S(1)}, f32[8,15,128]{1,0,2:T(8,128)}, u32[]{:S(2)}) copy-start(f32[8,15,128]{1,0,2:T(8,128)} %get-tuple-element.168) | copy-start | bytes 184324
  279.6 8.3 %copy-start.50 = (f32[8,15,128]{1,0,2:T(8,128)S(1)}, f32[8,15,128]{1,0,2:T(8,128)}, u32[]{:S(2)}) copy-start(f32[8,15,128]{1,0,2:T(8,128)} %get-tuple-element.169) | copy-start | bytes 184324
  281.9 13.5 %collective-permute-start.6 = (f32[2,4,16,128]{2,1,3,0:T(4,128)}, f32[2,4,16,128]{2,1,3,0:T(4,128)}, u32[]{:S(2)}, u32[]{:S(2)}) collective-permute-start(f32[2,4,16,128]{2,1,3,0:T(4,128)} %get-tuple-element.117), channel_id=1, source_target_pairs={{1,0},{2,1},{3,2},{4,3},{5,4},{6,5},{7,6},{8,7},{9,8},{10,9},{11,1... | collective-permute-start | bytes 196616 | tf_op jit(solution)/shard_map/ppermute | solution.py:28
  283.8 13.6 %collective-permute-start.7 = (f32[2,4,16,128]{2,1,3,0:T(4,128)}, f32[2,4,16,128]{2,1,3,0:T(4,128)}, u32[]{:S(2)}, u32[]{:S(2)}) collective-permute-start(f32[2,4,16,128]{2,1,3,0:T(4,128)} %get-tuple-element.116), channel_id=1, source_target_pairs={{0,1},{1,2},{2,3},{3,4},{4,5},{5,6},{6,7},{7,8},{8,9},{9,10},{10,1... | collective-permute-start | bytes 196616 | tf_op jit(solution)/shard_map/ppermute | solution.py:26
  322.4 8.4 %copy-start.69 = (f32[2,8,16,128]{2,1,3,0:T(8,128)S(1)}, f32[2,8,16,128]{2,1,3,0:T(8,128)}, u32[]{:S(2)}) copy-start(f32[2,8,16,128]{2,1,3,0:T(8,128)} %copy.616) | copy-start | bytes 393220
  337.3 8.2 %copy-start.111 = (f32[1,8,16,128]{3,2,1,0:T(8,128)S(1)}, f32[1,8,16,128]{3,2,1,0:T(8,128)}, u32[]{:S(2)}) copy-start(f32[1,8,16,128]{3,2,1,0:T(8,128)} %get-tuple-element.251) | copy-start | bytes 196612
  (92 other events, 514.3 us)
where the time goes:
time: 371 us; the launch traced here: 364 us
  local copies, waits for them, and re-layouts  196 us (53%)
  other arithmetic  124 us (33%)
  starting transfers between devices  30.9 us (8%)
  waiting for transfers between devices  10.5 us (3%)
    slice x50, local copies, waits for them, and re-layouts, window(): lax.slice_in_dim(array_in, begin_at, begin_at + extent, axis=direction)  74.5 us
    slice x36, local copies, waits for them, and re-layouts, moved(): lax.slice_in_dim(field, offset, length, axis=direction)  55.5 us
    unnamed x278, local copies, waits for them, and re-layouts  39.4 us
    another operation x21, other arithmetic, advance(): return (jnp.stack([p_next, q_next]), (slope_x, slope_y, slope_z))  30.1 us
    add x4, other arithmetic, first_along(): summed + first_coeffs[offset - 1] * (moved(field, direction, offset) - mo...  26.4 us
    add x4, other arithmetic, advance(): cosine * cosine * second_z + sine * sine * second_x  22.9 us
    ppermute x4, starting transfers between devices, padded_2(): lax.ppermute(tail, axis, [(i, (i + 1) % count) for i in range(ends)])  16.7 us
    mul x2, other arithmetic, angle_image(): scaled = (cosine + 1.0) * (0.5 * (FINE - 1))  9.83 us
  transfers between devices with their start and end apart: 9, of which 3 were waited for; matrix products, arithmetic and copies ran while one was open for 62% of the time, Pallas kernels for 0%

commit v1 on v0

v1 whole, which is shorter than its diff:
```python
import functools

import jax
import jax.numpy as jnp
from jax import lax
from jax.experimental import pallas as pl
from jax.experimental.pallas import tpu as pltpu
from jax.sharding import PartitionSpec as P

STEPS = 4
IMAGE_EVERY = 2
NBIN = 8
FINE = 32
REC_DEPTH = 2
REACH = 4
GROUP = 4

second_coeffs = (-205.0 / 72.0, 8.0 / 5.0, -1.0 / 5.0, 8.0 / 315.0, -1.0 / 560.0)
first_coeffs = (4.0 / 5.0, -1.0 / 5.0, 4.0 / 105.0, -1.0 / 280.0)
MESH = pl.DeviceIdType.MESH


def shifted_pairs(f, axis):
    size = f.shape[axis]
    place = lax.broadcasted_iota(jnp.int32, f.shape, axis)
    pairs = []
    for k in range(1, REACH + 1):
        ahead = jnp.where(place < size - k, pltpu.roll(f, size - k, axis), 0.0)
        behind = jnp.where(place >= k, pltpu.roll(f, k, axis), 0.0)
        pairs.append((ahead, behind))
    return pairs


def second_of(f, pairs):
    total = second_coeffs[0] * f
    for k, (ahead, behind) in enumerate(pairs):
        total = total + second_coeffs[k + 1] * (ahead + behind)
    return total


def first_of(pairs):
    total = None
    for k, (ahead, behind) in enumerate(pairs):
        term = first_coeffs[k] * (ahead - behind)
        total = term if total is None else total + term
    return total


def row_pairs(ref, lead, start):
    return [
        (
            ref[lead + (pl.ds(start + REACH + k, GROUP),)],
            ref[lead + (pl.ds(start + REACH - k, GROUP),)],
        )
        for k in range(1, REACH + 1)
    ]


def kernel(
    n,
    now_hbm, prev_hbm, speed_hbm, eps_hbm, delta_hbm, tilt_hbm, source_hbm,
    rows_ref, cols_ref, traces_ref, table_ref,
    images_ref, final_ref,
    pad, prev, med, coef, source, staged, arrived, snap, slopes, aim, inject, base, slope_z,
    in_sem, halo_send, halo_recv, all_send, all_recv,
):
    me = lax.axis_index("gx")
    nx, ny, nz = prev.shape[1:]
    local_ny = source.shape[2]
    has_left, has_right = me > 0, me < n - 1
    left, right = lax.rem(me + n - 1, n), lax.rem(me + 1, n)
    own = pl.ds(REACH, nx)
    far = REACH + nx

    barrier = pltpu.get_barrier_semaphore()

    def greet(k, carry):
        pl.semaphore_signal(
            barrier, inc=1, device_id={"gx": lax.rem(me + k, n)}, device_id_type=MESH
        )
        return carry

    lax.fori_loop(1, n, greet, 0)

    loads = [
        pltpu.make_async_copy(source_hbm, source, in_sem.at[0]),
        pltpu.make_async_copy(tilt_hbm, med.at[0], in_sem.at[1]),
        pltpu.make_async_copy(speed_hbm, med.at[1], in_sem.at[2]),
        pltpu.make_async_copy(eps_hbm, med.at[2], in_sem.at[3]),
        pltpu.make_async_copy(delta_hbm, med.at[3], in_sem.at[4]),
        pltpu.make_async_copy(now_hbm, pad.at[0, :, own], in_sem.at[5]),
        pltpu.make_async_copy(prev_hbm, prev, in_sem.at[6]),
    ]
    for load in loads:
        load.start()

    def halo_left(t):
        source_of = now_hbm.at[:, pl.ds(0, REACH)] if t == 0 else pad.at[t, :, pl.ds(REACH, REACH)]
        return pltpu.make_async_remote_copy(
            src_ref=source_of,
            dst_ref=pad.at[t, :, pl.ds(far, REACH)],
            send_sem=halo_send.at[t, 0],
            recv_sem=halo_recv.at[t, 1],
            device_id={"gx": left},
            device_id_type=MESH,
        )

    def halo_right(t):
        source_of = (
            now_hbm.at[:, pl.ds(nx - REACH, REACH)] if t == 0 else pad.at[t, :, pl.ds(nx, REACH)]
        )
        return pltpu.make_async_remote_copy(
            src_ref=source_of,
            dst_ref=pad.at[t, :, pl.ds(0, REACH)],
            send_sem=halo_send.at[t, 1],
            recv_sem=halo_recv.at[t, 0],
            device_id={"gx": right},
            device_id_type=MESH,
        )

    def block_to(j, k, target, slot):
        return pltpu.make_async_remote_copy(
            src_ref=staged.at[j, target],
            dst_ref=arrived.at[j, pl.ds(slot * local_ny, local_ny)],
            send_sem=all_send.at[j, k],
            recv_sem=all_recv.at[j, k],
            device_id={"gx": target},
            device_id_type=MESH,
        )

    def send_blocks(j):
        def send(k, carry):
            block_to(j, k, lax.rem(me + k, n), me).start()
            return carry

        lax.fori_loop(1, n, send, 0)
        arrived[j, pl.ds(me * local_ny, local_ny)] = staged[j, me]

    def take_blocks(j):
        def take(k, carry):
            block_to(j, k, lax.rem(me + k, n), lax.rem(me + n - k, n)).wait_recv()
            return carry

        lax.fori_loop(1, n, take, 0)

    def sent_blocks(j):
        def sent(k, carry):
            block_to(j, k, lax.rem(me + k, n), me).wait_send()
            return carry

        lax.fori_loop(1, n, sent, 0)

    pl.semaphore_wait(barrier, n - 1)

    @pl.when(has_left)
    def _():
        halo_left(0).start()

    @pl.when(has_right)
    def _():
        halo_right(0).start()

    for t in range(STEPS):
        @pl.when(me == 0)
        def _():
            pad[t, :, pl.ds(0, REACH)] = jnp.zeros((2, REACH, ny, nz), jnp.float32)

        @pl.when(me == n - 1)
        def _():
            pad[t, :, pl.ds(far, REACH)] = jnp.zeros((2, REACH, ny, nz), jnp.float32)

    loads[0].wait()
    for j in range(source.shape[0]):
        for y in range(local_ny):
            for c in range(4):
                whole = source[j, c, y].astype(jnp.float32).reshape(n, nx, nz)
                snap[c, pl.ds(0, n)] = whole
            joined = jnp.concatenate([snap[c, pl.ds(0, n)] for c in range(4)], axis=1)
            staged[j, :, y] = joined.astype(jnp.bfloat16)
        if j == 0:
            send_blocks(0)

    for load in loads[1:5]:
        load.wait()
    for i in range(0, nx, GROUP):
        rows = pl.ds(i, GROUP)
        tilt = med[0, rows]
        cosine = jnp.cos(tilt)
        sine = jnp.sin(tilt)
        speed = med[1, rows]
        ratio = jnp.sqrt(1.0 + 2.0 * med[3, rows])
        coef[0, rows] = cosine * cosine
        coef[1, rows] = sine * sine
        coef[2, rows] = 2.0 * sine * cosine
        coef[3, rows] = speed * (1.0 + 2.0 * med[2, rows])
        coef[4, rows] = speed * ratio
        coef[5, rows] = speed

    first_row = me * nx
    at_column = cols_ref[...] == lax.broadcasted_iota(jnp.int32, (ny, cols_ref.shape[1]), 0)
    at_depth = lax.broadcasted_iota(jnp.int32, (ny, nz), 1) == REC_DEPTH

    def one_row(x, carry):
        here = jnp.where(rows_ref[...] == first_row + x, traces_ref[...], 0.0)
        for t in range(STEPS):
            summed = jnp.sum(
                jnp.where(at_column, here[t : t + 1], 0.0), axis=1, keepdims=True
            )
            inject[t, x] = jnp.where(at_depth, summed, 0.0)
        return carry

    lax.fori_loop(0, nx, one_row, 0)

    for load in loads[5:]:
        load.wait()

    def before(t):
        imaging = t % IMAGE_EVERY == IMAGE_EVERY - 1
        for i in range(0, nx, GROUP):
            rows = pl.ds(i, GROUP)
            p = pad[t, 0, pl.ds(REACH + i, GROUP)]
            q = pad[t, 1, pl.ds(REACH + i, GROUP)]
            p_old = prev[0, rows] if t == 0 else pad[t - 1, 0, pl.ds(REACH + i, GROUP)]
            q_old = prev[1, rows] if t == 0 else pad[t - 1, 1, pl.ds(REACH + i, GROUP)]
            pairs = shifted_pairs(p, 2)
            slope = first_of(pairs)
            slope_z[0, pl.ds(REACH + i, GROUP)] = slope
            p_zz = second_of(p, pairs)
            pairs = shifted_pairs(q, 2)
            slope_z[1, pl.ds(REACH + i, GROUP)] = first_of(pairs)
            q_zz = second_of(q, pairs)
            pairs = shifted_pairs(p, 1)
            p_yy = second_of(p, pairs)
            if imaging:
                j = t // IMAGE_EVERY
                slopes[j, 1, rows] = first_of(pairs)
                slopes[j, 2, rows] = slope
            across = coef[1, rows] * p_zz + p_yy
            rotated = coef[0, rows] * q_zz
            base[0, rows] = (
                2.0 * p - p_old + inject[t, rows]
                + (coef[3, rows] * across + coef[4, rows] * rotated)
            )
            base[1, rows] = (
                2.0 * q - q_old + (coef[4, rows] * across + coef[5, rows] * rotated)
            )

    def after(t):
        imaging = t % IMAGE_EVERY == IMAGE_EVERY - 1
        last = t == STEPS - 1

        @pl.when(has_left)
        def _():
            halo_left(t).wait_send()
            halo_right(t).wait_recv()

        @pl.when(has_right)
        def _():
            halo_right(t).wait_send()
            halo_left(t).wait_recv()

        for start in (0, far):
            for f in range(2):
                rows = pl.ds(start, REACH)
                slope_z[f, rows] = first_of(shifted_pairs(pad[t, f, rows], 2))
        for i in range(0, nx, GROUP):
            rows = pl.ds(i, GROUP)
            middle = pl.ds(REACH + i, GROUP)
            pairs = row_pairs(pad, (t, 0), i)
            p_xx = second_of(pad[t, 0, middle], pairs)
            if imaging:
                slopes[t // IMAGE_EVERY, 0, rows] = first_of(pairs)
            q_xx = second_of(pad[t, 1, middle], row_pairs(pad, (t, 1), i))
            p_xz = first_of(row_pairs(slope_z, (0,), i))
            q_xz = first_of(row_pairs(slope_z, (1,), i))
            across = coef[0, rows] * p_xx - coef[2, rows] * p_xz
            rotated = coef[1, rows] * q_xx + coef[2, rows] * q_xz
            p_new = base[0, rows] + (coef[3, rows] * across + coef[4, rows] * rotated)
            q_new = base[1, rows] + (coef[4, rows] * across + coef[5, rows] * rotated)
            if last:
                final_ref[0, rows] = p_new
                final_ref[1, rows] = q_new
            else:
                pad[t + 1, 0, middle] = p_new
                pad[t + 1, 1, middle] = q_new
                if i == 0:
                    @pl.when(has_left)
                    def _():
                        halo_left(t + 1).start()

                if i + GROUP == nx:
                    @pl.when(has_right)
                    def _():
                        halo_right(t + 1).start()

    def angles(j):
        t = j * IMAGE_EVERY + IMAGE_EVERY - 1
        take_blocks(j)
        blocks = arrived[j].astype(jnp.float32)
        for c in range(4):
            snap[c] = blocks[:, c * nx : (c + 1) * nx]
        for x in range(nx):
            s, fx, fy, fz = (
                snap.at[c].reshape(ny * nx, nz)[pl.ds(x, ny, stride=nx), :] for c in range(4)
            )
            p = pad[t, 0, REACH + x]
            rate = p - pad[t - 1, 0, REACH + x]
            gx = -rate * slopes[j, 0, x]
            gy = -rate * slopes[j, 1, x]
            gz = -rate * slopes[j, 2, x]
            inner = fx * gx + fy * gy + fz * gz
            lengths = jnp.sqrt(fx * fx + fy * fy + fz * fz) * jnp.sqrt(gx * gx + gy * gy + gz * gz)
            cosine = inner / jnp.maximum(lengths, 1.0)
            aim[j, 0, x] = (cosine + 1.0) * (0.5 * (FINE - 1))
            aim[j, 1, x] = s * p

    before(0)
    after(0)
    send_blocks(1)
    before(1)
    after(1)
    before(2)
    after(2)
    before(3)
    angles(0)
    after(3)
    angles(1)

    table = table_ref[...]
    lower = [
        jnp.sum((table < b).astype(jnp.float32), axis=1, keepdims=True) for b in range(NBIN + 1)
    ]
    for x in range(nx):
        uses = [(aim[j, 0, x], aim[j, 1, x]) for j in range(STEPS // IMAGE_EVERY)]
        above = [jnp.clip(u - lower[0] + 1.0, 0.0, 1.0) for u, _ in uses]
        for b in range(NBIN):
            beyond = [jnp.clip(u - lower[b + 1] + 1.0, 0.0, 1.0) for u, _ in uses]
            total = None
            for (_, w), low, high in zip(uses, above, beyond):
                term = (low - high) * w
                total = term if total is None else total + term
            images_ref[b, x] = total.astype(jnp.bfloat16)
            above = beyond
    sent_blocks(0)
    sent_blocks(1)


def local(
    n,
    wave_now,
    wave_prev,
    speed_term,
    thomsen_epsilon,
    thomsen_delta,
    tilt_angle,
    source_store,
    receiver_row,
    receiver_column,
    receiver_traces,
    angle_table,
):
    fields, nx, ny, nz = wave_now.shape
    snaps, parts, whole_x, local_ny, _ = source_store.shape
    padded_x = nx + 2 * REACH
    f32, bf16 = jnp.float32, jnp.bfloat16
    hbm = pl.BlockSpec(memory_space=pl.ANY)
    vmem = pl.BlockSpec(memory_space=pltpu.VMEM)
    return pl.pallas_call(
        functools.partial(kernel, n),
        out_shape=(
            jax.ShapeDtypeStruct((NBIN, nx, ny, nz), bf16),
            jax.ShapeDtypeStruct((fields, nx, ny, nz), f32),
        ),
        in_specs=[hbm] * 7 + [vmem] * 4,
        out_specs=(vmem, vmem),
        scratch_shapes=[
            pltpu.VMEM((STEPS, fields, padded_x, ny, nz), f32),
            pltpu.VMEM((fields, nx, ny, nz), f32),
            pltpu.VMEM((4, nx, ny, nz), f32),
            pltpu.VMEM((6, nx, ny, nz), f32),
            pltpu.VMEM((snaps, parts, local_ny, whole_x, nz), bf16),
            pltpu.VMEM((snaps, n, local_ny, parts * nx, nz), bf16),
            pltpu.VMEM((snaps, ny, parts * nx, nz), bf16),
            pltpu.VMEM((parts, ny, nx, nz), f32),
            pltpu.VMEM((snaps, 3, nx, ny, nz), f32),
            pltpu.VMEM((snaps, 2, nx, ny, nz), f32),
            pltpu.VMEM((STEPS, nx, ny, nz), f32),
            pltpu.VMEM((fields, nx, ny, nz), f32),
            pltpu.VMEM((fields, padded_x, ny, nz), f32),
            pltpu.SemaphoreType.DMA((7,)),
            pltpu.SemaphoreType.DMA((STEPS, 2)),
            pltpu.SemaphoreType.DMA((STEPS, 2)),
            pltpu.SemaphoreType.DMA((snaps, n)),
            pltpu.SemaphoreType.DMA((snaps, n)),
        ],
        compiler_params=pltpu.CompilerParams(
            collective_id=0, has_side_effects=True, vmem_limit_bytes=48 * 1024 * 1024
        ),
    )(
        wave_now,
        wave_prev,
        speed_term,
        thomsen_epsilon,
        thomsen_delta,
        tilt_angle,
        source_store.transpose(0, 1, 3, 2, 4),
        receiver_row.reshape(1, -1),
        receiver_column.reshape(1, -1),
        receiver_traces,
        angle_table.reshape(1, -1),
    )


def solution(mesh):
    placed = (
        P("shot", "gx", None, None),
        P("shot", "gx", None, None),
        P("gx", None, None),
        P("gx", None, None),
        P("gx", None, None),
        P("gx", None, None),
        P("shot", None, None, "gx", None),
        P("shot"),
        P("shot"),
        P("shot", None),
        P(),
    )
    return jax.shard_map(
        functools.partial(local, mesh.shape["gx"]),
        mesh=mesh,
        in_specs=placed,
        out_specs=(P("shot", "gx", None, None), P("shot", "gx", None, None)),
        check_vma=False,
    )
```

time: 371 us -> 31.9 us (0.09); the launches traced: 364 us -> 31.5 us
  local copies, waits for them, and re-layouts: 196 us -> 8.14 us
  other arithmetic: 124 us -> 0 us
  starting transfers between devices: 30.9 us -> 0 us
  Pallas kernels: 0 us -> 22.7 us
  waiting for transfers between devices: 10.5 us -> 0 us
    slice x88 -> x0, local copies, waits for them, and re-layouts: 132 us -> none  [the longest x50 74.5 us: window(): lax.slice_in_dim(array_in, begin_at, begin_at + extent, axis=direction)]
    add x14 -> x0, other arithmetic: 60.2 us -> none  [the longest x4 26.4 us: first_along(): summed + first_coeffs[offset - 1] * (moved(field, direction, offset) - mo...]
    unnamed x278 -> x24, local copies, waits for them, and re-layouts: 39.4 us -> 8.14 us
    another operation x21 -> x0, other arithmetic: 30.1 us -> none  [advance(): return (jnp.stack([p_next, q_next]), (slope_x, slope_y, slope_z))]
    ppermute x8 -> x0, starting transfers between devices: 24.5 us -> none  [the longest x4 16.7 us: padded_2(): lax.ppermute(tail, axis, [(i, (i + 1) % count) for i in range(ends)])]
    pallas_call x0 -> x1, Pallas kernels: none -> 22.7 us  [local(): pl.pallas_call(functools.partial(kernel, n), out_shape=(jax.ShapeDtypeStr...]
    mul x5 -> x0, other arithmetic: 13.1 us -> none  [the longest x2 9.83 us: angle_image(): scaled = (cosine + 1.0) * (0.5 * (FINE - 1))]
    ppermute x8 -> x0, waiting for transfers between devices: 10.5 us -> none  [the longest x4 8.17 us: padded_2(): lax.ppermute(tail, axis, [(i, (i + 1) % count) for i in range(ends)])]
  transfers between devices with their start and end apart: 9 -> 0, of which waited for: 3 -> 0; matrix products, arithmetic and copies ran while one was open for 62% -> 0% of each run, Pallas kernels for 0% -> 0%
where the time goes in v1:
time: 31.9 us; the launch traced here: 31.5 us
  Pallas kernels  22.7 us (71%)
  local copies, waits for them, and re-layouts  8.14 us (26%)
  between operations  0.68 us (2%)
    pallas_call x1, Pallas kernels, local(): pl.pallas_call(functools.partial(kernel, n), out_shape=(jax.ShapeDtypeStr...  22.7 us
    unnamed x24, local copies, waits for them, and re-layouts  8.14 us

profile of v1, /device:TPU:1, one launch (start us, length us, event | category | flops | bytes accessed | tf_op | source)
XLA Modules:
  0.0 31.5 jit_solution(17154057952165884589)
XLA Ops:
  0.6 0.0 copy-start.7
  0.6 0.0 copy-start.8
  0.7 0.0 copy-start.9
  0.7 0.0 copy-start.10
  0.7 0.6 %copy-done.7 = f32[4,128]{1,0:T(4,128)S(1)} copy-done((f32[4,128]{1,0:T(4,128)S(1)}, f32[4,128]{1,0:T(4,128)}, u32[]{:S(2)}) %copy-start.7) | copy-done | bytes 2072
  1.3 0.0 copy-done.8
  1.3 0.0 copy-done.9
  1.3 0.0 copy-done.10
  1.3 0.0 copy-start
  1.3 0.9 %copy-done = bf16[2,4,128,1,128]{4,2,3,1,0:T(8,128)(2,1)S(1)} copy-done((bf16[2,4,128,1,128]{4,2,3,1,0:T(8,128)(2,1)S(1)}, bf16[2,4,128,1,128]{4,2,3,1,0:T(8,128)(2,1)}, u32[]{:S(2)}) %copy-start) | copy-done | bytes 262168
  2.3 0.0 copy-start.1
  2.3 0.9 %copy-done.1 = f32[2,8,16,128]{3,2,1,0:T(8,128)S(1)} copy-done((f32[2,8,16,128]{3,2,1,0:T(8,128)S(1)}, f32[2,8,16,128]{3,2,1,0:T(8,128)}, u32[]{:S(2)}) %copy-start.1) | copy-done | bytes 131096
  3.2 0.0 copy-start.2
  3.2 0.9 %copy-done.2 = f32[2,8,16,128]{3,2,1,0:T(8,128)S(1)} copy-done((f32[2,8,16,128]{3,2,1,0:T(8,128)S(1)}, f32[2,8,16,128]{3,2,1,0:T(8,128)}, u32[]{:S(2)}) %copy-start.2) | copy-done | bytes 131096
  4.1 0.0 copy-start.3
  4.1 0.8 %copy-done.3 = f32[8,16,128]{2,1,0:T(8,128)S(1)} copy-done((f32[8,16,128]{2,1,0:T(8,128)S(1)}, f32[8,16,128]{2,1,0:T(8,128)}, u32[]{:S(2)}) %copy-start.3) | copy-done | bytes 65560
  4.9 0.0 copy-start.4
  4.9 0.8 %copy-done.4 = f32[8,16,128]{2,1,0:T(8,128)S(1)} copy-done((f32[8,16,128]{2,1,0:T(8,128)S(1)}, f32[8,16,128]{2,1,0:T(8,128)}, u32[]{:S(2)}) %copy-start.4) | copy-done | bytes 65560
  5.8 0.0 copy-start.5
  5.8 0.8 %copy-done.5 = f32[8,16,128]{2,1,0:T(8,128)S(1)} copy-done((f32[8,16,128]{2,1,0:T(8,128)S(1)}, f32[8,16,128]{2,1,0:T(8,128)}, u32[]{:S(2)}) %copy-start.5) | copy-done | bytes 65560
  6.6 0.0 copy-start.6
  6.6 0.8 %copy-done.6 = f32[8,16,128]{2,1,0:T(8,128)S(1)} copy-done((f32[8,16,128]{2,1,0:T(8,128)S(1)}, f32[8,16,128]{2,1,0:T(8,128)}, u32[]{:S(2)}) %copy-start.6) | copy-done | bytes 65560
  7.5 22.7 %shard_map.122 = (bf16[8,8,16,128]{3,2,1,0:T(8,128)(2,1)S(1)}, f32[2,8,16,128]{3,2,1,0:T(8,128)S(1)}) custom-call(f32[2,8,16,128]{3,2,1,0:T(8,128)S(1)} %copy-done.1, f32[2,8,16,128]{3,2,1,0:T(8,128)S(1)} %copy-done.2, f32[8,16,128]{2,1,0:T(8,128)S(1)} %copy-done.3, f32[8,16,128]{2,1,0:T(8,128)S(1)} %copy-done.4, f32[8,16,128]{2,1,0:T(8,128)S(1)} %copy-done.5, ...), custom_call_target="tpu_custom_call" | custom-call | tf_op jit(solution)/shard_map/pallas_call | solution.py:368
  30.1 0.7 %copy.15 = bf16[8,8,16,128]{3,2,1,0:T(8,128)(2,1)} copy(bf16[8,8,16,128]{3,2,1,0:T(8,128)(2,1)S(1)} %get-tuple-element.4) | data formatting | bytes 524288
  30.9 0.7 %copy.16 = f32[2,8,16,128]{3,2,1,0:T(8,128)} copy(f32[2,8,16,128]{3,2,1,0:T(8,128)S(1)} %get-tuple-element.5) | data formatting | bytes 262144
Async XLA Ops:
  0.6 0.7 %copy-start.7 = (f32[4,128]{1,0:T(4,128)S(1)}, f32[4,128]{1,0:T(4,128)}, u32[]{:S(2)}) copy-start(f32[4,128]{1,0:T(4,128)} %traces_ref.1) | copy-start | bytes 6148
  0.6 0.7 %copy-start.8 = (s32[128]{0:T(128)S(1)}, s32[128]{0:T(128)}, u32[]{:S(2)}) copy-start(s32[128]{0:T(128)} %param.18) | copy-start | bytes 1540
  0.7 0.7 %copy-start.9 = (s32[128]{0:T(128)S(1)}, s32[128]{0:T(128)}, u32[]{:S(2)}) copy-start(s32[128]{0:T(128)} %param.19) | copy-start | bytes 1540
  0.7 0.7 %copy-start.10 = (s32[32]{0:T(128)S(1)}, s32[32]{0:T(128)}, u32[]{:S(2)}) copy-start(s32[32]{0:T(128)} %param.21) | copy-start | bytes 388
  1.3 0.9 %copy-start = (bf16[2,4,128,1,128]{4,2,3,1,0:T(8,128)(2,1)S(1)}, bf16[2,4,128,1,128]{4,2,3,1,0:T(8,128)(2,1)}, u32[]{:S(2)}) copy-start(bf16[2,4,128,1,128]{4,2,3,1,0:T(8,128)(2,1)} %param.17) | copy-start | bytes 786436
  2.3 0.9 %copy-start.1 = (f32[2,8,16,128]{3,2,1,0:T(8,128)S(1)}, f32[2,8,16,128]{3,2,1,0:T(8,128)}, u32[]{:S(2)}) copy-start(f32[2,8,16,128]{3,2,1,0:T(8,128)} %now_hbm.1) | copy-start | bytes 393220
  3.2 0.9 %copy-start.2 = (f32[2,8,16,128]{3,2,1,0:T(8,128)S(1)}, f32[2,8,16,128]{3,2,1,0:T(8,128)}, u32[]{:S(2)}) copy-start(f32[2,8,16,128]{3,2,1,0:T(8,128)} %prev_hbm.1) | copy-start | bytes 393220
  4.1 0.8 %copy-start.3 = (f32[8,16,128]{2,1,0:T(8,128)S(1)}, f32[8,16,128]{2,1,0:T(8,128)}, u32[]{:S(2)}) copy-start(f32[8,16,128]{2,1,0:T(8,128)} %speed_hbm.1) | copy-start | bytes 196612
  4.9 0.8 %copy-start.4 = (f32[8,16,128]{2,1,0:T(8,128)S(1)}, f32[8,16,128]{2,1,0:T(8,128)}, u32[]{:S(2)}) copy-start(f32[8,16,128]{2,1,0:T(8,128)} %eps_hbm.1) | copy-start | bytes 196612
  5.8 0.8 %copy-start.5 = (f32[8,16,128]{2,1,0:T(8,128)S(1)}, f32[8,16,128]{2,1,0:T(8,128)}, u32[]{:S(2)}) copy-start(f32[8,16,128]{2,1,0:T(8,128)} %delta_hbm.1) | copy-start | bytes 196612
  6.6 0.8 %copy-start.6 = (f32[8,16,128]{2,1,0:T(8,128)S(1)}, f32[8,16,128]{2,1,0:T(8,128)}, u32[]{:S(2)}) copy-start(f32[8,16,128]{2,1,0:T(8,128)} %tilt_hbm.1) | copy-start | bytes 196612

commit v2 on v1

--- a/solution.py
+++ b/solution.py
@@ -59,9 +59,10 @@
 def kernel(
     n,
     now_hbm, prev_hbm, speed_hbm, eps_hbm, delta_hbm, tilt_hbm, source_hbm,
-    rows_ref, cols_ref, traces_ref, table_ref,
+    rows_hbm, cols_hbm, traces_hbm, table_hbm,
     images_ref, final_ref,
     pad, prev, med, coef, source, staged, arrived, snap, slopes, aim, inject, base, slope_z,
+    rows_ref, cols_ref, traces_ref, table_ref,
     in_sem, halo_send, halo_recv, all_send, all_recv,
 ):
     me = lax.axis_index("gx")
@@ -88,6 +89,10 @@
         pltpu.make_async_copy(speed_hbm, med.at[1], in_sem.at[2]),
         pltpu.make_async_copy(eps_hbm, med.at[2], in_sem.at[3]),
         pltpu.make_async_copy(delta_hbm, med.at[3], in_sem.at[4]),
+        pltpu.make_async_copy(rows_hbm, rows_ref, in_sem.at[7]),
+        pltpu.make_async_copy(cols_hbm, cols_ref, in_sem.at[8]),
+        pltpu.make_async_copy(traces_hbm, traces_ref, in_sem.at[9]),
+        pltpu.make_async_copy(table_hbm, table_ref, in_sem.at[10]),
         pltpu.make_async_copy(now_hbm, pad.at[0, :, own], in_sem.at[5]),
         pltpu.make_async_copy(prev_hbm, prev, in_sem.at[6]),
     ]
@@ -150,16 +155,6 @@
 
         lax.fori_loop(1, n, sent, 0)
 
-    pl.semaphore_wait(barrier, n - 1)
-
-    @pl.when(has_left)
-    def _():
-        halo_left(0).start()
-
-    @pl.when(has_right)
-    def _():
-        halo_right(0).start()
-
     for t in range(STEPS):
         @pl.when(me == 0)
         def _():
@@ -169,18 +164,7 @@
         def _():
             pad[t, :, pl.ds(far, REACH)] = jnp.zeros((2, REACH, ny, nz), jnp.float32)
 
-    loads[0].wait()
-    for j in range(source.shape[0]):
-        for y in range(local_ny):
-            for c in range(4):
-                whole = source[j, c, y].astype(jnp.float32).reshape(n, nx, nz)
-                snap[c, pl.ds(0, n)] = whole
-            joined = jnp.concatenate([snap[c, pl.ds(0, n)] for c in range(4)], axis=1)
-            staged[j, :, y] = joined.astype(jnp.bfloat16)
-        if j == 0:
-            send_blocks(0)
-
-    for load in loads[1:5]:
+    for load in loads[1:9]:
         load.wait()
     for i in range(0, nx, GROUP):
         rows = pl.ds(i, GROUP)
@@ -211,7 +195,27 @@
 
     lax.fori_loop(0, nx, one_row, 0)
 
-    for load in loads[5:]:
+    pl.semaphore_wait(barrier, n - 1)
+
+    @pl.when(has_left)
+    def _():
+        halo_left(0).start()
+
+    @pl.when(has_right)
+    def _():
+        halo_right(0).start()
+
+    def stage(j):
+        for y in range(local_ny):
+            for c in range(4):
+                snap[c, pl.ds(0, n)] = source[j, c, y].astype(jnp.float32).reshape(n, nx, nz)
+            joined = jnp.concatenate([snap[c, pl.ds(0, n)] for c in range(4)], axis=1)
+            staged[j, :, y] = joined.astype(jnp.bfloat16)
+        send_blocks(j)
+
+    loads[0].wait()
+    stage(0)
+    for load in loads[9:]:
         load.wait()
 
     def before(t):
@@ -316,8 +320,8 @@
 
     before(0)
     after(0)
-    send_blocks(1)
     before(1)
+    stage(1)
     after(1)
     before(2)
     after(2)
@@ -363,7 +367,7 @@
     snaps, parts, whole_x, local_ny, _ = source_store.shape
     padded_x = nx + 2 * REACH
     f32, bf16 = jnp.float32, jnp.bfloat16
-    hbm = pl.BlockSpec(memory_space=pl.ANY)
+    hbm = pl.BlockSpec(memory_space=pltpu.HBM)
     vmem = pl.BlockSpec(memory_space=pltpu.VMEM)
     return pl.pallas_call(
         functools.partial(kernel, n),
@@ -371,7 +375,7 @@
             jax.ShapeDtypeStruct((NBIN, nx, ny, nz), bf16),
             jax.ShapeDtypeStruct((fields, nx, ny, nz), f32),
         ),
-        in_specs=[hbm] * 7 + [vmem] * 4,
+        in_specs=[hbm] * 11,
         out_specs=(vmem, vmem),
         scratch_shapes=[
             pltpu.VMEM((STEPS, fields, padded_x, ny, nz), f32),
@@ -387,14 +391,18 @@
             pltpu.VMEM((STEPS, nx, ny, nz), f32),
             pltpu.VMEM((fields, nx, ny, nz), f32),
             pltpu.VMEM((fields, padded_x, ny, nz), f32),
-            pltpu.SemaphoreType.DMA((7,)),
+            pltpu.VMEM((1, receiver_row.shape[0]), jnp.int32),
+            pltpu.VMEM((1, receiver_row.shape[0]), jnp.int32),
+            pltpu.VMEM(receiver_traces.shape, f32),
+            pltpu.VMEM((1, angle_table.shape[0]), jnp.int32),
+            pltpu.SemaphoreType.DMA((11,)),
             pltpu.SemaphoreType.DMA((STEPS, 2)),
             pltpu.SemaphoreType.DMA((STEPS, 2)),
             pltpu.SemaphoreType.DMA((snaps, n)),
             pltpu.SemaphoreType.DMA((snaps, n)),
         ],
         compiler_params=pltpu.CompilerParams(
-            collective_id=0, has_side_effects=True, vmem_limit_bytes=48 * 1024 * 1024
+            collective_id=0, has_side_effects=True, vmem_limit_bytes=62914560
         ),
     )(
         wave_now,

time: 31.9 us -> 27 us (0.85)
  local copies, waits for them, and re-layouts: 8.14 us -> 2.37 us
  Pallas kernels: 22.7 us -> 23.9 us
    unnamed x24 -> x4, local copies, waits for them, and re-layouts: 8.14 us -> 2.37 us
    pallas_call x1, Pallas kernels: 22.7 us -> 23.9 us  [local(): pl.pallas_call(functools.partial(kernel, n), out_shape=(jax.ShapeDtypeStr...]
where the time goes in v2:
time: 27 us; the launch traced here: 26.9 us
  Pallas kernels  23.9 us (89%)
  local copies, waits for them, and re-layouts  2.37 us (9%)
  between operations  0.65 us (2%)
    pallas_call x1, Pallas kernels, local(): pl.pallas_call(functools.partial(kernel, n), out_shape=(jax.ShapeDtypeStr...  23.9 us
    unnamed x4, local copies, waits for them, and re-layouts  2.37 us

profile of v2, /device:TPU:1, one launch (start us, length us, event | category | flops | bytes accessed | tf_op | source)
XLA Modules:
  0.0 26.9 jit_solution(16511110223531130009)
XLA Ops:
  0.6 23.9 %shard_map.122 = (bf16[8,8,16,128]{3,2,1,0:T(8,128)(2,1)}, f32[2,8,16,128]{3,2,1,0:T(8,128)}) custom-call(f32[2,8,16,128]{3,2,1,0:T(8,128)} %now_hbm.1, f32[2,8,16,128]{3,2,1,0:T(8,128)} %prev_hbm.1, f32[8,16,128]{2,1,0:T(8,128)} %speed_hbm.1, f32[8,16,128]{2,1,0:T(8,128)} %eps_hbm.1, f32[8,16,128]{2,1,0:T(8,128)} %delta_hbm.1, f32[8,16,128]{2,1,0:T(8,128)} %tilt_hbm.1, ...), custom_call_target="tpu_custom_call" | custom-call | tf_op jit(solution)/shard_map/pallas_call | solution.py:372
  24.5 0.0 copy-start
  24.5 1.7 %copy.15 = bf16[8,8,16,128]{3,2,1,0:T(8,128)(2,1)} copy(bf16[8,8,16,128]{3,2,1,0:T(8,128)(2,1)} %get-tuple-element.4) | data formatting | bytes 524288
  26.2 0.0 copy-done
  26.2 0.7 %copy.16 = f32[2,8,16,128]{3,2,1,0:T(8,128)} copy(f32[2,8,16,128]{3,2,1,0:T(8,128)S(1)} %copy-done) | data formatting | bytes 262144
Async XLA Ops:
  24.5 1.7 %copy-start = (f32[2,8,16,128]{3,2,1,0:T(8,128)S(1)}, f32[2,8,16,128]{3,2,1,0:T(8,128)}, u32[]{:S(2)}) copy-start(f32[2,8,16,128]{3,2,1,0:T(8,128)} %get-tuple-element.5) | copy-start | bytes 393220

commit v3 on v2

--- a/solution.py
+++ b/solution.py
@@ -195,16 +195,6 @@
 
     lax.fori_loop(0, nx, one_row, 0)
 
-    pl.semaphore_wait(barrier, n - 1)
-
-    @pl.when(has_left)
-    def _():
-        halo_left(0).start()
-
-    @pl.when(has_right)
-    def _():
-        halo_right(0).start()
-
     def stage(j):
         for y in range(local_ny):
             for c in range(4):
@@ -213,8 +203,6 @@
             staged[j, :, y] = joined.astype(jnp.bfloat16)
         send_blocks(j)
 
-    loads[0].wait()
-    stage(0)
     for load in loads[9:]:
         load.wait()
 
@@ -319,6 +307,18 @@
             aim[j, 1, x] = s * p
 
     before(0)
+    pl.semaphore_wait(barrier, n - 1)
+
+    @pl.when(has_left)
+    def _():
+        halo_left(0).start()
+
+    @pl.when(has_right)
+    def _():
+        halo_right(0).start()
+
+    loads[0].wait()
+    stage(0)
     after(0)
     before(1)
     stage(1)

time: 27 us -> 26.8 us (level)
  Pallas kernels: 23.9 us -> 23.6 us
where the time goes in v3:
time: 26.8 us; the launch traced here: 26.7 us
  Pallas kernels  23.6 us (88%)
  local copies, waits for them, and re-layouts  2.37 us (9%)
  between operations  0.65 us (2%)
    pallas_call x1, Pallas kernels, local(): pl.pallas_call(functools.partial(kernel, n), out_shape=(jax.ShapeDtypeStr...  23.6 us
    unnamed x4, local copies, waits for them, and re-layouts  2.37 us

profile of v3, /device:TPU:1, one launch (start us, length us, event | category | flops | bytes accessed | tf_op | source)
XLA Modules:
  0.0 26.7 jit_solution(4589474521716950498)
XLA Ops:
  0.6 23.6 %shard_map.122 = (bf16[8,8,16,128]{3,2,1,0:T(8,128)(2,1)}, f32[2,8,16,128]{3,2,1,0:T(8,128)}) custom-call(f32[2,8,16,128]{3,2,1,0:T(8,128)} %now_hbm.1, f32[2,8,16,128]{3,2,1,0:T(8,128)} %prev_hbm.1, f32[8,16,128]{2,1,0:T(8,128)} %speed_hbm.1, f32[8,16,128]{2,1,0:T(8,128)} %eps_hbm.1, f32[8,16,128]{2,1,0:T(8,128)} %delta_hbm.1, f32[8,16,128]{2,1,0:T(8,128)} %tilt_hbm.1, ...), custom_call_target="tpu_custom_call" | custom-call | tf_op jit(solution)/shard_map/pallas_call | solution.py:372
  24.3 0.0 copy-start
  24.3 1.7 %copy.15 = bf16[8,8,16,128]{3,2,1,0:T(8,128)(2,1)} copy(bf16[8,8,16,128]{3,2,1,0:T(8,128)(2,1)} %get-tuple-element.4) | data formatting | bytes 524288
  26.0 0.0 copy-done
  26.0 0.7 %copy.16 = f32[2,8,16,128]{3,2,1,0:T(8,128)} copy(f32[2,8,16,128]{3,2,1,0:T(8,128)S(1)} %copy-done) | data formatting | bytes 262144
Async XLA Ops:
  24.3 1.7 %copy-start = (f32[2,8,16,128]{3,2,1,0:T(8,128)S(1)}, f32[2,8,16,128]{3,2,1,0:T(8,128)}, u32[]{:S(2)}) copy-start(f32[2,8,16,128]{3,2,1,0:T(8,128)} %get-tuple-element.5) | copy-start | bytes 393220
